TPU v7x, 256 devices: a whole 4x4x8 slice. The times are simulated.
256 devices in a mesh: role: 2 (over z_lo), dp: 4 (over y), vocab: 32 (over z_hi, x, core).
Axes of the slice: x: 4, y: 4, z: 8 (z_hi: 4, z_lo: 2; z = z_hi * 2 + z_lo), core: 2. Of those that a mesh axis runs over, the one named last changes fastest.
Arguments:
- hidden: bfloat16 [4096, 1792], P(('role', 'dp'))
- out_weight: bfloat16 [1792, 77824], P(None, 'vocab')
- teacher_logits: bfloat16 [4096, 77824], P(('role', 'dp'), 'vocab')
- token_ids: int32 [4096], P(('role', 'dp')), may hold values from 0 to 77823
- loss_mask: int32 [4096], P(('role', 'dp')), may hold values from 0 to 1
Outputs:
- token_kl: float32 [4096], P(('role', 'dp'))
- chosen_logprob: float32 [4096], P(('role', 'dp'))
- grad_hidden: bfloat16 [4096, 1792], P(('role', 'dp', 'vocab'))
- grad_weight: bfloat16 [1792, 77824], P(('role', 'dp'), 'vocab')
All inputs are finite; a program needn't handle non-finite values.
Results may differ from a plain program's by a relative error of at most 0.02.
Values may be sent and summed in bfloat16 or wider, within the bound.
A program may use at most 128 MiB of HBM per device.

v0:
```python
import jax
import jax.numpy as jnp
from jax import lax
from jax.sharding import PartitionSpec as P


def from_partner(shard, axis, bit):
    return lax.ppermute(shard, axis, [(i, i ^ 1 << bit) for i in range(lax.axis_size(axis))])


def local(hidden, out_weight, teacher_logits, token_ids, loss_mask):
    shard_width = out_weight.shape[1]
    teacher_tile = from_partner(teacher_logits, "role", 0)
    logits = jnp.dot(hidden, out_weight, preferred_element_type=jnp.float32)
    mask_values = loss_mask.astype(jnp.float32)
    mask_total = jnp.maximum(lax.psum(jnp.sum(mask_values), ("role", "dp")), 1.0)
    columns = lax.axis_index("vocab") * shard_width + lax.iota(jnp.int32, shard_width)
    pick_local = jnp.sum(jnp.where(token_ids[:, None] == columns[None, :], logits, 0.0), axis=1)
    teacher = teacher_tile.astype(jnp.float32)
    logit_gap = logits - teacher
    student_top, teacher_top = lax.pmax(
        (jnp.max(logits, axis=1), jnp.max(teacher, axis=1)), "vocab"
    )
    shifted = jnp.exp(logits - student_top[:, None])
    student_sum, gap_sum, teacher_sum, picked = lax.psum(
        (
            jnp.sum(shifted, axis=1),
            jnp.sum(shifted * logit_gap, axis=1),
            jnp.sum(jnp.exp(teacher - teacher_top[:, None]), axis=1),
            pick_local,
        ),
        "vocab",
    )
    lse_student = student_top + jnp.log(student_sum)
    lse_teacher = teacher_top + jnp.log(teacher_sum)
    lse_diff = lse_student - lse_teacher
    token_kl = gap_sum / student_sum - lse_diff
    chosen_logprob = picked - lse_student
    probs = jnp.exp(logits - lse_student[:, None])
    grad_logits = (
        (mask_values / mask_total)[:, None]
        * probs
        * (logit_gap - lse_diff[:, None] - token_kl[:, None])
    ).astype(jnp.bfloat16)
    block = grad_logits
    grad_hidden = lax.psum_scatter(
        lax.dot_general(
            block, out_weight, (((1,), (1,)), ((), ())), preferred_element_type=jnp.float32
        ).astype(jnp.bfloat16),
        "vocab",
        scatter_dimension=0,
        tiled=True,
    )
    block = hidden
    grad_weight = lax.psum_scatter(
        lax.dot_general(
            block, grad_logits, (((0,), (0,)), ((), ())), preferred_element_type=jnp.float32
        ).astype(jnp.bfloat16),
        ("role", "dp"),
        scatter_dimension=0,
        tiled=True,
    )
    return (token_kl, chosen_logprob, grad_hidden, grad_weight)


def solution(mesh):
    return jax.shard_map(
        local,
        mesh=mesh,
        in_specs=(
            P(("role", "dp"), None),
            P(None, "vocab"),
            P(("role", "dp"), "vocab"),
            P(("role", "dp")),
            P(("role", "dp")),
        ),
        out_specs=(
            P(("role", "dp")),
            P(("role", "dp")),
            P(("role", "dp", "vocab"), None),
            P(("role", "dp"), "vocab"),
        ),
        check_vma=False,
    )
```

profile of v0, /device:TPU:1, one launch (start us, length us, event | category | flops | bytes accessed | tf_op | source)
XLA Modules:
  0.0 445.3 jit_solution(4842880105465729757)
XLA Ops:
  7.2 0.0 copy-start
  7.2 0.0 reduce-scatter.5.cloned.1.call-start
  7.2 2.6 collective-permute-start
  9.8 1.3 convert_reduce_fusion
  11.1 63.1 %psum.39 = f32[]{:T(128)} all-reduce(f32[]{:T(128)} %convert_reduce_fusion), channel_id=1, replica_groups=mesh['role'=2,'dp'=4,'vocab'=32] {'role','dp'}, use_global_device_ids=true, to_apply=%region_13.14 | all-reduce | flops 1 | bytes 8 | tf_op jit(solution)/shard_map/psum | solution.py:16
  74.8 0.7 convert_divide_fusion
  75.5 0.0 copy-done
  75.5 10.2 %fusion.5 = (f32[512]{0:T(512)S(1)}, f32[512,2432]{1,0:T(8,128)}) fusion(bf16[512,1792]{1,0:T(8,128)(2,1)S(1)} %copy-done, bf16[1792,2432]{1,0:T(8,128)(2,1)} %param.6), kind=kOutput, calls=%fused_computation.19 | convolution fusion | flops 4463984128 | bytes 15534080 | tf_op jit(solution)/shard_map/dot_general | solution.py:14
  85.7 0.0 collective-permute-done
  85.7 2.1 reduce_max.24
  87.8 75.2 %all-reduce.1 = (f32[512]{0:T(512)S(1)}, f32[512]{0:T(512)S(1)}) all-reduce(f32[512]{0:T(512)S(1)} %get-tuple-element.26, bf16[512]{0:T(512)(128)(2,1)S(1)} %reduce_max.24), channel_id=1, replica_groups=mesh['role'=2,'dp'=4,'vocab'=32] {'vocab'}, use_global_device_ids=true, to_apply=%region_1.0 | all-reduce | flops 1024 | bytes 7168 | tf_op jit(solution)/shard_map/pmax | solution.py:21
  163.0 0.0 copy-done.1
  163.0 5.0 %multiply_reduce_fusion = (f32[512]{0:T(512)S(1)}, f32[512]{0:T(512)S(1)}, f32[512]{0:T(512)S(1)}, f32[512]{0:T(512)S(1)}) fusion(f32[512,2432]{1,0:T(8,128)} %get-tuple-element.27, bf16[512,2432]{1,0:T(8,128)(2,1)} %collective-permute-done, f32[512]{0:T(512)S(1)} %get-tuple-element.20, s32[2432]{0:T(1024)S(1)} %iota_add_fusion, s32[512]{0:T(512)S(1)} %copy-done.1, ...), kind=kLoop, calls=%fused_computation.8 | loop fusion | flops 13694976 | bytes 7495168 | tf_op jit(solution)/shard_map/reduce_sum | solution.py:28
  168.1 72.4 %all-reduce = (f32[512]{0:T(512)S(1)}, f32[512]{0:T(512)S(1)}, f32[512]{0:T(512)S(1)}, f32[512]{0:T(512)S(1)}) all-reduce(f32[512]{0:T(512)S(1)} %get-tuple-element.13, f32[512]{0:T(512)S(1)} %get-tuple-element.15, f32[512]{0:T(512)S(1)} %get-tuple-element.12, ...), channel_id=1, replica_groups=mesh['role'=2,'dp'=4,'vocab'=32] {'vocab'}, use_global_device_ids=true, to_apply=%region_5.6 | all-reduce | flops 2048 | bytes 16384 | tf_op jit(solution)/shard_map/psum | solution.py:25
  240.4 0.6 fusion.4
  241.0 12.7 %convolution_convert_fusion.1 = bf16[512,1792]{1,0:T(8,128)(2,1)} fusion(bf16[1792,2432]{1,0:T(8,128)(2,1)} %param.6, f32[512,2432]{1,0:T(8,128)} %get-tuple-element.27, bf16[512,2432]{1,0:T(8,128)(2,1)} %collective-permute-done, f32[512]{0:T(512)S(1)} %get-tuple-element.24, f32[512]{0:T(512)S(1)} %get-tuple-element.25, f32[512]{0:T(512)S(1)} %get-tuple-element.23, ...), kind=kOutput, calls=%fused_computation.11 | convolution fusion | flops 4473618432 | bytes 18030592 | tf_op jit(solution)/shard_map/dot_general | solution.py:47
  253.7 0.0 reduce-scatter.5.cloned.1.call-update
  253.7 0.2 reduce-scatter.7.cloned.1.call-start
  254.0 0.0 copy-done.2
  254.0 12.5 %fusion = bf16[1792,2432]{0,1:T(8,128)(2,1)} fusion(bf16[512,1792]{1,0:T(8,128)(2,1)S(1)} %copy-done, f32[512,2432]{1,0:T(8,128)} %get-tuple-element.27, bf16[512,2432]{1,0:T(8,128)(2,1)} %collective-permute-done, f32[512]{0:T(512)S(1)} %get-tuple-element.24, f32[512]{0:T(512)S(1)} %get-tuple-element.25, f32[512]{0:T(512)S(1)} %get-tuple-element.23, ...), kind=kOutput, calls=%fused_computation.1 | convolution fusion | flops 4477059072 | bytes 18030592 | tf_op jit(solution)/shard_map/dot_general | solution.py:56
  266.5 12.6 %copy.11 = bf16[1792,2432]{1,0:T(8,128)(2,1)} copy(bf16[1792,2432]{0,1:T(8,128)(2,1)} %fusion) | data formatting | bytes 17432576
  279.1 0.0 reduce-scatter.7.cloned.1.call-update
  279.1 58.1 %reduce-scatter.5.cloned.1.call-done = bf16[16,1792]{1,0:T(8,128)(2,1)} async-done(((bf16[512,1792]{1,0:T(8,128)(2,1)}), bf16[16,1792]{1,0:T(8,128)(2,1)}) %reduce-scatter.5.cloned.1.call-update) | async-done | bytes 57360 | tf_op jit(solution)/shard_map/reduce_scatter | solution.py:46
  337.2 101.2 %reduce-scatter.7.cloned.1.call-done = bf16[224,2432]{1,0:T(8,128)(2,1)} async-done(((bf16[1792,2432]{1,0:T(8,128)(2,1)}), bf16[224,2432]{1,0:T(8,128)(2,1)}) %reduce-scatter.7.cloned.1.call-update) | async-done | bytes 1089552
  (4 shorter events, 0.0 us)
Async XLA Ops:
  7.2 68.3 %copy-start = (bf16[512,1792]{1,0:T(8,128)(2,1)S(1)}, bf16[512,1792]{1,0:T(8,128)(2,1)}, u32[]{:S(2)}) copy-start(bf16[512,1792]{1,0:T(8,128)(2,1)} %param.5) | copy-start | bytes 5505028
  7.2 330.0 %reduce-scatter.5.cloned.1.call-start = ((), (), s32[]{:S(2)}) async-start(), calls=%async_computation.2 | async-start | bytes 1892352 | tf_op jit(solution)/shard_map/reduce_scatter | solution.py:46
  7.2 78.5 %collective-permute-start = (bf16[512,2432]{1,0:T(8,128)(2,1)}, bf16[512,2432]{1,0:T(8,128)(2,1)}, u32[]{:S(2)}, u32[]{:S(2)}) collective-permute-start(bf16[512,2432]{1,0:T(8,128)(2,1)} %param.7), channel_id=1, source_target_pairs={{0,128},{128,0},{1,129},{129,1},{2,130},{130,2},{3,131},{131,3},{4... | collective-permute-start | bytes 7471112 | tf_op jit(solution)/shard_map/ppermute | solution.py:8
  75.5 87.5 %copy-start.1 = (s32[512]{0:T(512)S(1)}, s32[512]{0:T(512)}, u32[]{:S(2)}) copy-start(s32[512]{0:T(512)} %param.8) | copy-start | bytes 6148
  241.0 12.9 %copy-start.2 = (f32[512]{0:T(512)}, f32[512]{0:T(512)S(1)}, u32[]{:S(2)}) copy-start(f32[512]{0:T(512)S(1)} %get-tuple-element.24) | copy-start | bytes 6148
  253.7 184.7 %reduce-scatter.7.cloned.1.call-start = ((), (), s32[]{:S(2)}) async-start(), calls=%async_computation.3 | async-start | bytes 9805824
Sparse Core Ops, SparseCore 0:
  253.9 83.2 reduce-scatter.4
  340.4 98.0 reduce-scatter.6
where the time goes:
time: 446 us; the launch traced here: 445 us
  blocking collectives  211 us (47%)
  waiting for transfers between devices  159 us (36%)
  matrix products  35.4 us (8%)
  between operations  14.7 us (3%)
  local copies, waits for them, and re-layouts  12.6 us (3%)
  other arithmetic  9.74 us (2%)
    unnamed x3, waiting for transfers between devices  101 us
    pmax x1, blocking collectives, local(): lax.pmax((jnp.max(logits, axis=1), jnp.max(teacher, axis=1)), 'vocab')  75.2 us
    psum x1, blocking collectives, local(): lax.psum((jnp.sum(shifted, axis=1), jnp.sum(shifted * logit_gap, axis=1),...  72.4 us
    psum x1, blocking collectives, local(): lax.psum(jnp.sum(mask_values), ('role', 'dp'))  63.1 us
    reduce_scatter x1, waiting for transfers between devices, local(): lax.psum_scatter(lax.dot_general(block, out_weight, (((1,), (1,)), ((), (...  58.1 us
    dot_general x1, matrix products, local(): lax.dot_general(block, out_weight, (((1,), (1,)), ((), ())), preferred_el...  12.7 us
    unnamed x7, local copies, waits for them, and re-layouts  12.6 us
    dot_general x1, matrix products, local(): lax.dot_general(block, grad_logits, (((0,), (0,)), ((), ())), preferred_e...  12.5 us
  transfers between devices with their start and end apart: 3, of which 2 were waited for; matrix products, arithmetic and copies ran while one was open for 8% of the time, Pallas kernels for 0%

commit v1 on v0

v1 whole, which is shorter than its diff:
```python
import functools

import jax
import jax.numpy as jnp
from jax import lax
from jax.experimental import pallas as pl
from jax.experimental.pallas import tpu as pltpu
from jax.sharding import PartitionSpec as P

F32 = jnp.float32
BF16 = jnp.bfloat16
MESH = pl.DeviceIdType.MESH

TOK = 512
H = 1792
VW = 2432
LANE = 128
TILES = VW // LANE
NJ = 5
BLK = NJ * LANE
CH = 256
HALF = H // 2
ROWS = 224


def _rows(i, n):
    return pl.ds(pl.multiple_of(i * n, n), n)


def kernel_body(
    hidden, weight, teacher, ids, mask,
    kl_out, chosen_out, gh_out, gw_out,
    wv, tv, hall, first, rest, logits, lmax, sacc, tacc, idb, coef, gown, grecv,
    st1, st1r, st2, st2r, fin, fin_r, meta, meta_r, cnt, cnt_r,
    zs, zr, wacc, fs, idv, mkv, klv, chv, gh, gha, gb, gbr, gc, gcr, gd,
    lsem, ssem, rsem,
):
    r = lax.axis_index("role")
    d = lax.axis_index("dp")
    v = lax.axis_index("vocab")
    zh = lax.div(v, 8)
    x = lax.rem(lax.div(v, 2), 4)
    c = lax.rem(v, 2)

    def dev(r_, d_, zh_, x_, c_):
        return (r_, d_, (zh_ * 4 + x_) * 2 + c_)

    def plus(a, o):
        return lax.rem(a + o, 4)

    def along_z(o):
        z = lax.rem(zh * 2 + r + o, 8)
        return dev(lax.rem(z, 2), d, lax.div(z, 2), x, c)

    z_up, z_down = along_z(1), along_z(7)
    mate = dev(1 - r, d, zh, x, c)
    core = dev(r, d, zh, x, 1 - c)
    dp_peer = [None] + [dev(r, plus(d, o), zh, x, c) for o in (1, 2, 3)]
    x_peer = [None] + [dev(r, d, zh, plus(x, o), c) for o in (1, 2, 3)]
    zh_peer = [None] + [dev(r, d, plus(zh, o), x, c) for o in (1, 2, 3)]
    xc_peer = [None] + [dev(r, d, zh, plus(x, o), 1 - c) for o in (1, 2, 3)]

    count = [0]
    pending = []

    def remote(src, dst, to):
        i = count[0]
        count[0] += 1
        cp = pltpu.make_async_remote_copy(
            src_ref=src, dst_ref=dst, send_sem=ssem.at[i], recv_sem=rsem.at[i],
            device_id=to, device_id_type=MESH,
        )
        return cp

    def send(src, dst, to):
        cp = remote(src, dst, to)
        cp.start()
        pending.append(cp)
        return cp

    def sent(cps):
        for cp in cps:
            cp.wait_send()
            pending[:] = [q for q in pending if q is not cp]

    load_w = pltpu.make_async_copy(weight, wv, lsem.at[0])
    load_t = pltpu.make_async_copy(teacher, tv, lsem.at[1])
    load_i = pltpu.make_async_copy(ids, idv, lsem.at[2 + NJ])
    load_m = pltpu.make_async_copy(mask, mkv, lsem.at[3 + NJ])
    load_i.start()
    load_m.start()
    load_t.start()
    load_w.start()

    barrier = pltpu.get_barrier_semaphore()
    partners = [z_up, z_down, core] + dp_peer[1:] + x_peer[1:] + zh_peer[1:] + xc_peer[1:]
    for p in partners:
        pl.semaphore_signal(barrier, inc=1, device_id=p, device_id_type=MESH)
    load_i.wait()
    load_m.wait()
    meta[...] = jnp.concatenate(
        [mkv[...].astype(F32), idv[...].astype(F32), jnp.zeros((6, TOK), F32)], axis=0
    )
    pl.semaphore_wait(barrier, len(partners))

    def send_own(k):
        base = pl.multiple_of(k * CH + c * 128, 128)
        up = pl.ds(base, 64)
        down = pl.ds(pl.multiple_of(base + 64, 64), 64)
        return [
            send(hidden.at[up], hall.at[0, up], z_up),
            send(hidden.at[down], hall.at[0, down], z_down),
        ]

    meta_cp = send(meta, meta_r, mate)
    own = [send_own(0)]
    first_rows = hidden.at[pl.ds(pl.multiple_of(c * 128 + x * 32, 32), 32)]
    first_cp = [send(first_rows, first.at[o - 1], dp_peer[o]) for o in (1, 2, 3)]

    load_t.wait()

    def teacher_stats(i, _):
        rows = _rows(i, 64)
        m = tv[rows, 0:LANE]
        for j in range(1, TILES):
            m = jnp.maximum(m, tv[rows, j * LANE:(j + 1) * LANE])
        m = jnp.broadcast_to(jnp.max(m.astype(F32), axis=1, keepdims=True), (64, LANE))
        s = jnp.zeros((64, LANE), F32)
        for j in range(TILES):
            s = s + jnp.exp(tv[rows, j * LANE:(j + 1) * LANE].astype(F32) - m)
        tacc[0, rows, :] = m
        tacc[1, rows, :] = s
        return 0

    lax.fori_loop(0, TOK // 64, teacher_stats, 0)

    others = pl.ds(1, 3)

    def cross(cps, buf, row, n):
        for cp in cps:
            cp.wait_recv()
        out = []
        for i, to in enumerate((z_up, z_down)):
            rows = pl.ds(pl.multiple_of(row + i * n, n), n)
            out.append(send(buf.at[:, pl.ds(i * n, n)], hall.at[others, rows], to))
        return out

    rest_rows = hidden.at[pl.ds(pl.multiple_of(CH + c * 128 + 64, 64), 64)]
    rest_cp = [send(rest_rows, rest.at[o - 1], dp_peer[o]) for o in (1, 2, 3)]
    sent(own[0])
    own.append(send_own(1))

    meta_cp.wait_recv()
    both = meta[0:1, :] + meta_r[0:1, :]
    part = both[:, 0:128] + both[:, 128:256] + both[:, 256:384] + both[:, 384:512]
    cnt[...] = jnp.broadcast_to(part, (8, LANE))
    cnt_cp = [send(cnt, cnt_r.at[o - 1], dp_peer[o]) for o in (1, 2, 3)]
    id_cols = jnp.concatenate([meta_r[...], jnp.zeros((120, TOK), F32)], axis=0).T
    idb[...] = jnp.broadcast_to(id_cols[:, 1:2], (TOK, LANE)) - (v * VW).astype(F32)

    load_w.wait()

    def piece(k, x_):
        n = 32 if k == 0 else 16
        return pl.ds(pl.multiple_of(k * CH + c * 128 + x_ * n, 16), n)

    def core_rows(k):
        return pl.ds(pl.multiple_of(k * CH + c * 128, 128), 128)

    left_cols, right_cols = pl.ds(0, HALF), pl.ds(HALF, HALF)

    def core_own(k):
        for cp in own[k]:
            cp.wait_recv()
        fwd = send(hall.at[0, core_rows(k)], hall.at[0, core_rows(k)], core)
        if k == 0:
            return fwd, None
        mine = piece(k, x)
        return fwd, [send(hall.at[0, mine], hall.at[o, mine], dp_peer[o]) for o in (1, 2, 3)]

    def x_first(k, ys):
        for cp in ys:
            cp.wait_recv()
        mine = piece(k, x)
        return [
            send(hall.at[others, mine], hall.at[others, mine], x_peer[1]),
            send(hall.at[others, mine], hall.at[others, mine], x_peer[3]),
        ]

    def x_second(k, xs):
        out = []
        for cp, o, cols in zip(xs, (3, 1), (left_cols, right_cols)):
            cp.wait_recv()
            theirs = hall.at[others, piece(k, plus(x, o)), cols]
            out.append(send(theirs, theirs, x_peer[4 - o]))
        return out

    def forward_core(k, xs):
        for cp in xs:
            cp.wait_recv()
        rows = hall.at[others, core_rows(k)]
        return send(rows, rows, core)

    def logit_tile(k, first, width, start):
        rs = slice(k * CH, (k + 1) * CH)
        cols = pl.ds(first, width)
        l = jnp.dot(hall[0, rs, :], wv[:, cols], preferred_element_type=F32)
        logits[rs, cols] = l
        m = l[:, 0:LANE] if start else jnp.maximum(lmax[rs, :], l[:, 0:LANE])
        for q in range(1, width // LANE):
            m = jnp.maximum(m, l[:, q * LANE:(q + 1) * LANE])
        lmax[rs, :] = m

    def logits_chunk(k):
        logit_tile(k, 0, LANE, True)

        def body(n, _):
            logit_tile(k, pl.multiple_of(n * 768 + LANE, LANE), 768, False)
            return 0

        lax.fori_loop(0, 3, body, 0)

    def student_stats(k):
        def body(i, _):
            rows = pl.ds(pl.multiple_of(k * CH + i * 64, 64), 64)
            m = jnp.broadcast_to(jnp.max(lmax[rows, :], axis=1, keepdims=True), (64, LANE))
            token = idb[rows, :]
            lane = lax.broadcasted_iota(jnp.int32, (64, LANE), 1).astype(F32)
            s = jnp.zeros((64, LANE), F32)
            g = s
            picked = s
            for j in range(TILES):
                cols = slice(j * LANE, (j + 1) * LANE)
                l = logits[rows, cols]
                t = tv[rows, cols].astype(F32)
                e = jnp.exp(l - m)
                s = s + e
                g = g + e * (l - t)
                picked = picked + jnp.where(lane == token - float(j * LANE), l, 0.0)
            sacc[0, rows, :] = m
            sacc[1, rows, :] = s
            sacc[2, rows, :] = g
            sacc[3, rows, :] = picked
            return 0

        lax.fori_loop(0, CH // 64, body, 0)
        rs = slice(k * CH, (k + 1) * CH)

        def total(a):
            return jnp.sum(a.T, axis=0, keepdims=True)

        st1[k] = jnp.concatenate(
            [
                sacc[0, rs, :].T[0:1], total(sacc[1, rs, :]), total(sacc[2, rs, :]),
                total(sacc[3, rs, :]), tacc[0, rs, :].T[0:1], total(tacc[1, rs, :]),
                jnp.zeros((2, CH), F32),
            ],
            axis=0,
        )
        cps = [send(st1.at[k], st1r.at[k, 0], core)]
        for o in (1, 2, 3):
            cps.append(send(st1.at[k], st1r.at[k, o], x_peer[o]))
            cps.append(send(st1.at[k], st1r.at[k, 3 + o], xc_peer[o]))
        return cps

    def combine(msgs):
        top = functools.reduce(jnp.maximum, [m[0:1] for m in msgs])
        ttop = functools.reduce(jnp.maximum, [m[4:5] for m in msgs])
        s = g = pk = ts = None
        for m in msgs:
            w = jnp.exp(m[0:1] - top)
            tw = jnp.exp(m[4:5] - ttop)
            a, b, p, t = w * m[1:2], w * m[2:3], m[3:4], tw * m[5:6]
            s, g, pk, ts = (a, b, p, t) if s is None else (s + a, g + b, pk + p, ts + t)
        return top, s, g, pk, ttop, ts

    def stats_second(k, cps):
        for cp in cps:
            cp.wait_recv()
        rows = combine([st1[k]] + [st1r[k, i] for i in range(7)])
        st2[k] = jnp.concatenate(list(rows) + [jnp.zeros((2, CH), F32)], axis=0)
        return [send(st2.at[k], st2r.at[k, o - 1], zh_peer[o]) for o in (1, 2, 3)]

    def stats_final(k, cps):
        for cp in cps:
            cp.wait_recv()
        top, s, g, pk, ttop, ts = combine([st2[k]] + [st2r[k, i] for i in range(3)])
        lse = top + jnp.log(s)
        lse_t = ttop + jnp.log(ts)
        mean_gap = g / s
        rs = slice(k * CH, (k + 1) * CH)
        fin[k] = jnp.concatenate(
            [mean_gap - (lse - lse_t), pk - lse, jnp.zeros((6, CH), F32)], axis=0
        )
        scale = meta_r[0:1, rs] / mask_total
        cols = jnp.concatenate([lse, mean_gap, scale, jnp.zeros((125, CH), F32)], axis=0).T
        for i in range(3):
            coef[i, rs, :] = jnp.broadcast_to(cols[:, i:i + 1], (CH, LANE))
        return send(fin.at[k], fin_r.at[k], mate)

    def grad_tile(k, j):
        def body(i, _):
            rows = pl.ds(pl.multiple_of(k * CH + i * 64, 64), 64)
            lse, mean_gap, scale = coef[0, rows, :], coef[1, rows, :], coef[2, rows, :]
            for e in range(4):
                if e * NJ + j >= TILES:
                    continue
                cols = slice((e * NJ + j) * LANE, (e * NJ + j + 1) * LANE)
                l = logits[rows, cols]
                t = tv[rows, cols].astype(F32)
                grad = scale * jnp.exp(l - lse) * ((l - t) - mean_gap)
                gown[e, rows, j * LANE:(j + 1) * LANE] = grad.astype(BF16)
            return 0

        lax.fori_loop(0, CH // 64, body, 0)

    def g_copies(k, j):
        cps = []
        rs = pl.ds(0, TOK) if k is None else pl.ds(k * CH, CH)
        cs = pl.ds(j * LANE, LANE)
        for o in (1, 2, 3):
            e = plus(d, o)
            cps.append((remote(gown.at[e, rs, cs], grecv.at[o - 1, rs, cs], dp_peer[o]), e))
        return cps

    def g_each(u, what):
        for cp, e in gcp[u]:
            if u[1] < NJ - 1:
                getattr(cp, what)()
            else:
                pl.when(e < 3)(getattr(cp, what))

    def g_start(*u):
        gcp[u] = g_copies(*u)
        g_each(u, "start")

    def g_next(prev, u):
        g_each(prev, "wait_send")
        g_start(*u)

    def gh_chunk(k, first=0, last=H // 256):
        rs = slice(k * CH, (k + 1) * CH)

        def body(n, _):
            cols = _rows(n, 256)
            acc = None
            for e in range(4):
                width = min(BLK, VW - e * BLK)
                part_ = lax.dot_general(
                    gown[e, rs, 0:width], wv[cols, e * BLK:e * BLK + width],
                    (((1,), (1,)), ((), ())), preferred_element_type=F32,
                )
                acc = part_ if acc is None else acc + part_
            out = acc.astype(BF16)
            for u in range(16):
                w = k * 16 + u
                gh[w % 2, (w // 2) % 4, w // 8, :, cols] = out[u * 16:(u + 1) * 16]
            return 0

        lax.fori_loop(first, last, body, 0)

    fwd0, _ = core_own(0)
    cross0 = cross(first_cp, first, c * 128 + x * 32, 16)
    fwd0.wait_recv()
    logits_chunk(0)
    st1_0 = student_stats(0)
    xa0 = x_first(0, cross0)
    fwd1, ys1 = core_own(1)
    fwd1.wait_recv()
    logits_chunk(1)
    st1_1 = student_stats(1)
    st2_0 = stats_second(0, st1_0)
    xb0 = x_second(0, xa0)
    xa1 = x_first(1, ys1)
    for cp in cnt_cp:
        cp.wait_recv()
    mask_sum = cnt[...] + cnt_r[0] + cnt_r[1] + cnt_r[2]
    mask_total = jnp.maximum(jnp.sum(mask_sum[0:1], axis=1, keepdims=True), 1.0)
    st2_1 = stats_second(1, st1_1)
    last1 = cross(rest_cp, rest, CH + c * 128 + 64, 32)
    fin0 = stats_final(0, st2_0)
    gcp = {}
    grad_tile(0, 0)
    g_start(0, 0)
    grad_tile(0, 1)
    g_start(0, 1)
    for j in range(2, NJ):
        grad_tile(0, j)
    gh_chunk(0, 0, 6)
    fin1 = stats_final(1, st2_1)
    grad_tile(1, 0)
    g_start(1, 0)
    for j in range(1, NJ):
        grad_tile(1, j)
    cs0 = forward_core(0, xb0)
    xb1 = x_second(1, xa1)
    gh_chunk(0, 6, 7)
    g_start(1, 1)
    gh_chunk(1, 0, 5)
    cs1 = forward_core(1, xb1 + last1)
    gh_chunk(1, 5, 7)
    a_cp = send(gh.at[1 - c], gha, core)
    g_each((0, 0), "wait_send")
    g_next((1, 0), (None, 2))
    cs0.wait_recv()
    cs1.wait_recv()

    def weight_dot(half, j):
        cols = pl.ds(pl.multiple_of(half * HALF, LANE), HALF)
        cs = slice(j * LANE, (j + 1) * LANE)
        acc = None
        for o in range(4):
            g = gown[d, :, cs] if o == 0 else grecv[o - 1, :, cs]
            part_ = lax.dot_general(
                hall[o, :, cols], g, (((0,), (0,)), ((), ())), preferred_element_type=F32
            )
            acc = part_ if acc is None else acc + part_
        return acc

    def guarded(j, f):
        if j < NJ - 1:
            f()
        else:
            pl.when(d < 3)(f)

    def out_cols(j):
        d_ = d if j < NJ - 1 else lax.rem(d, 3)
        return pl.ds(pl.multiple_of(d_ * BLK + j * LANE, LANE), LANE)

    zcp = [remote(zs.at[j], zr.at[j], mate) for j in range(NJ)]
    fcp = [
        [
            remote(
                fs.at[j, plus(d, o)],
                gw_out.at[:, out_cols(j)],
                dp_peer[o],
            )
            for o in (1, 2, 3)
        ]
        for j in range(NJ)
    ]
    lcp = [
        pltpu.make_async_copy(
            fs.at[j, d],
            gw_out.at[:, out_cols(j)],
            lsem.at[2 + j],
        )
        for j in range(NJ)
    ]

    def weight_partial(j):
        def f():
            for u in ((0, j), (1, j)) if j < 2 else ((None, j),):
                for cp, _ in gcp[u]:
                    cp.wait_recv()
            zs[j] = weight_dot(1 - r, j).astype(BF16)
            if j > 0:
                zcp[j - 1].wait_send()
            zcp[j].start()
            wacc[j] = weight_dot(r, j)

        guarded(j, f)

    def weight_final(j):
        def f():
            zcp[j].wait_recv()
            for e in range(4):
                rs = slice(e * ROWS, (e + 1) * ROWS)
                fs[j, e] = (wacc[j, rs, :] + zr[j, rs, :].astype(F32)).astype(BF16)
            for cp in fcp[j]:
                cp.start()
            lcp[j].start()

        guarded(j, f)

    weight_partial(0)
    for k, cp in enumerate((fin0, fin1)):
        cp.wait_recv()
        rs = slice(k * CH, (k + 1) * CH)
        klv[:, rs] = fin_r[k, 0:1, :]
        chv[:, rs] = fin_r[k, 1:2, :]
    store_kl = pltpu.make_async_copy(klv, kl_out, lsem.at[4 + NJ])
    store_ch = pltpu.make_async_copy(chv, chosen_out, lsem.at[5 + NJ])
    store_kl.start()
    store_ch.start()
    a_cp.wait_recv()

    def add_a(i, _):
        gb[i] = (gh[c, i].astype(F32) + gha[i].astype(F32)).astype(BF16)
        return 0

    lax.fori_loop(0, 4, add_a, 0)
    b_cp = [send(gb.at[plus(x, o)], gbr.at[o - 1], x_peer[o]) for o in (1, 2, 3)]
    g_each((0, 1), "wait_send")
    g_next((1, 1), (None, 3))
    weight_partial(1)
    weight_final(0)
    g_next((None, 2), (None, 4))
    weight_partial(2)
    weight_final(1)
    for cp in b_cp:
        cp.wait_recv()
    for i in range(4):
        acc = gb[x, i].astype(F32)
        for o in range(3):
            acc = acc + gbr[o, i].astype(F32)
        gc[i] = acc.astype(BF16)
    c_cp = [send(gc.at[plus(zh, o)], gcr.at[o - 1], zh_peer[o]) for o in (1, 2, 3)]
    weight_partial(3)
    weight_final(2)
    weight_partial(4)
    weight_final(3)
    weight_final(4)
    for cp in c_cp:
        cp.wait_recv()
    acc = gc[zh].astype(F32)
    for o in range(3):
        acc = acc + gcr[o].astype(F32)
    gd[...] = acc.astype(BF16)
    d_cp = send(gd, gh_out, mate)

    d_cp.wait_recv()
    store_kl.wait()
    store_ch.wait()

    for cp in pending:
        cp.wait_send()
    for j in (3, 4):
        g_each((None, j), "wait_send")
    for j in range(NJ):
        def drain(j=j):
            if j == NJ - 1:
                zcp[j].wait_send()
            lcp[j].wait()
            for cp in fcp[j]:
                cp.wait_send()

        guarded(j, drain)
        if j == NJ - 2:
            pl.when(d == 3)(zcp[j].wait_send)
        for o in (1, 2, 3):
            if j < NJ - 1:
                fcp[j][o - 1].wait_recv()
            else:
                pl.when(plus(d, 4 - o) < 3)(fcp[j][o - 1].wait_recv)


N_COPIES = 140


def hand_on(a, b, c, d, a_out, b_out, c_out, d_out):
    a_out[...] = a[...]
    b_out[...] = b[...]
    c_out[...] = c[...]
    d_out[...] = d[...]


def local(hidden, out_weight, teacher_logits, token_ids, loss_mask):
    any_ = pl.BlockSpec(memory_space=pl.ANY)
    vm = pl.BlockSpec(memory_space=pltpu.VMEM)
    V = pltpu.VMEM
    outs = (
        jax.ShapeDtypeStruct((1, TOK), F32),
        jax.ShapeDtypeStruct((1, TOK), F32),
        jax.ShapeDtypeStruct((16, H), BF16),
        jax.ShapeDtypeStruct((ROWS, VW), BF16),
    )
    kl, chosen, grad_hidden, grad_weight = pl.pallas_call(
        kernel_body,
        out_shape=outs,
        in_specs=[any_] * 5,
        out_specs=(any_,) * 4,
        scratch_shapes=[
            V((H, VW), BF16),
            V((TOK, VW), BF16),
            V((4, TOK, H), BF16),
            V((3, 32, H), BF16),
            V((3, 64, H), BF16),
            V((TOK, VW), F32),
            V((TOK, LANE), F32),
            V((4, TOK, LANE), F32),
            V((2, TOK, LANE), F32),
            V((TOK, LANE), F32),
            V((3, TOK, LANE), F32),
            V((4, TOK, BLK), BF16),
            V((3, TOK, BLK), BF16),
            V((2, 8, CH), F32),
            V((2, 7, 8, CH), F32),
            V((2, 8, CH), F32),
            V((2, 3, 8, CH), F32),
            V((2, 8, CH), F32),
            V((2, 8, CH), F32),
            V((8, TOK), F32),
            V((8, TOK), F32),
            V((8, LANE), F32),
            V((3, 8, LANE), F32),
            V((NJ, HALF, LANE), BF16),
            V((NJ, HALF, LANE), BF16),
            V((NJ, HALF, LANE), F32),
            V((NJ, 4, ROWS, LANE), BF16),
            V((1, TOK), jnp.int32),
            V((1, TOK), jnp.int32),
            V((1, TOK), F32),
            V((1, TOK), F32),
            V((2, 4, 4, 16, H), BF16),
            V((4, 4, 16, H), BF16),
            V((4, 4, 16, H), BF16),
            V((3, 4, 16, H), BF16),
            V((4, 16, H), BF16),
            V((3, 16, H), BF16),
            V((16, H), BF16),
            pltpu.SemaphoreType.DMA((6 + NJ,)),
            pltpu.SemaphoreType.DMA((N_COPIES,)),
            pltpu.SemaphoreType.DMA((N_COPIES,)),
        ],
        compiler_params=pltpu.CompilerParams(
            collective_id=0, has_side_effects=True, vmem_limit_bytes=60 << 20
        ),
        cost_estimate=pl.CostEstimate(
            flops=6 * TOK * H * VW, bytes_accessed=16 << 20, transcendentals=3 * TOK * VW
        ),
        name="distill",
    )(hidden, out_weight, teacher_logits, token_ids.reshape(1, TOK), loss_mask.reshape(1, TOK))
    kl, chosen, grad_hidden, grad_weight = pl.pallas_call(
        hand_on,
        out_shape=outs,
        in_specs=[vm] * 4,
        out_specs=(vm,) * 4,
        name="handon",
    )(kl, chosen, grad_hidden, grad_weight)
    return kl.reshape(TOK), chosen.reshape(TOK), grad_hidden, grad_weight


def solution(mesh):
    return jax.shard_map(
        local,
        mesh=mesh,
        in_specs=(
            P(("role", "dp"), None),
            P(None, "vocab"),
            P(("role", "dp"), "vocab"),
            P(("role", "dp")),
            P(("role", "dp")),
        ),
        out_specs=(
            P(("role", "dp")),
            P(("role", "dp")),
            P(("role", "dp", "vocab"), None),
            P(("role", "dp"), "vocab"),
        ),
        check_vma=False,
    )
```

time: 446 us -> 92.6 us (0.21)
  blocking collectives: 211 us -> 0 us
  waiting for transfers between devices: 159 us -> 0 us
  Pallas kernels: 0 us -> 91.7 us
  matrix products: 35.4 us -> 0 us
  between operations: 14.7 us -> 0.64 us
  local copies, waits for them, and re-layouts: 12.6 us -> 0 us
  other arithmetic: 9.74 us -> 0 us
    psum x2 -> x0, blocking collectives: 135 us -> none  [the longest x1 72.4 us: local(): lax.psum((jnp.sum(shifted, axis=1), jnp.sum(shifted * logit_gap, axis=1),...]
    unnamed x3 -> x0, waiting for transfers between devices: 101 us -> none
    pallas_call x0 -> x2, Pallas kernels: none -> 91.7 us  [the longest x1 89.3 us: local(): pl.pallas_call(kernel_body, out_shape=outs, in_specs=[any_] * 5, out_spec...]
    pmax x1 -> x0, blocking collectives: 75.2 us -> none  [local(): lax.pmax((jnp.max(logits, axis=1), jnp.max(teacher, axis=1)), 'vocab')]
    reduce_scatter x1 -> x0, waiting for transfers between devices: 58.1 us -> none  [local(): lax.psum_scatter(lax.dot_general(block, out_weight, (((1,), (1,)), ((), (...]
    dot_general x3 -> x0, matrix products: 35.4 us -> none  [the longest x1 12.7 us: local(): lax.dot_general(block, out_weight, (((1,), (1,)), ((), ())), preferred_el...]
    unnamed x7 -> x0, local copies, waits for them, and re-layouts: 12.6 us -> none
    reduce_sum x2 -> x0, other arithmetic: 6.33 us -> none  [the longest x1 5.05 us: local(): jnp.sum(shifted * logit_gap, axis=1)]
  transfers between devices with their start and end apart: 3 -> 0, of which waited for: 2 -> 0; matrix products, arithmetic and copies ran while one was open for 8% -> 0% of each run, Pallas kernels for 0% -> 0%
where the time goes in v1:
time: 92.6 us; the launch traced here: 92.3 us
  Pallas kernels  91.7 us (99%)
    pallas_call x1, Pallas kernels, local(): pl.pallas_call(kernel_body, out_shape=outs, in_specs=[any_] * 5, out_spec...  89.3 us
    pallas_call x1, Pallas kernels, local(): pl.pallas_call(hand_on, out_shape=outs, in_specs=[vm] * 4, out_specs=(vm,...  2.35 us

profile of v1, /device:TPU:1, one launch (start us, length us, event | category | flops | bytes accessed | tf_op | source)
XLA Modules:
  0.0 92.3 jit_solution(12940696109625269071)
XLA Ops:
  0.6 89.3 %distill.1 = (f32[1,512]{1,0:T(1,128)}, f32[1,512]{1,0:T(1,128)}, bf16[16,1792]{1,0:T(8,128)(2,1)}, bf16[224,2432]{1,0:T(8,128)(2,1)}) custom-call(bf16[512,1792]{1,0:T(8,128)(2,1)} %hidden.1, bf16[1792,2432]{1,0:T(8,128)(2,1)} %weight.1, bf16[512,2432]{1,0:T(8,128)(2,1)} %teacher.1, s32[1,512]{1,0:T(1,128)} %bitcast.4, s32[1,512]{1,0:T(1,128)} %bitcast.5), custom_call_target="tpu_custom_call" | custom-call | flops 13388218368 | bytes 16777216 | tf_op jit(solution)/shard_map/distill/pallas_call | solution.py:568
  90.0 2.3 %handon.1 = (f32[1,512]{1,0:T(1,128)}, f32[1,512]{1,0:T(1,128)}, bf16[16,1792]{1,0:T(8,128)(2,1)}, bf16[224,2432]{1,0:T(8,128)(2,1)}) custom-call(f32[1,512]{1,0:T(1,128)} %get-tuple-element.12.a, f32[1,512]{1,0:T(1,128)} %get-tuple-element.13.b, bf16[16,1792]{1,0:T(8,128)(2,1)} %get-tuple-element.14.c, bf16[224,2432]{1,0:T(8,128)(2,1)} %get-tuple-element.15.d), custom_call_target="tpu_custom_call" | custom-call | tf_op jit(solution)/shard_map/handon/pallas_call | solution.py:624
